TPU v7x, 32 devices: a whole 2x2x4 slice. The times are simulated.
32 devices in a mesh: expert: 16 (over z, y, core), attn: 2 (over x).
Axes of the slice: x: 2, y: 2, z: 4, core: 2. Of those that a mesh axis runs over, the one named last changes fastest.
Arguments:
- queries: bfloat16 [512, 64, 576], P('expert', 'attn'), may hold values from -6 to 6
- prompt_cache: bfloat16 [64, 256, 576], P('expert'), may hold values from -6 to 6
- beam_cache: bfloat16 [512, 16, 576], P('expert'), may hold values from -6 to 6
- new_latent: bfloat16 [512, 576], P('expert'), may hold values from -6 to 6
- parents: int32 [512], P('expert'), may hold values from 0 to 7
- lengths: int32 [64], P('expert'), may hold values from 32 to 256, as said below
- up_values: bfloat16 [64, 512, 128], P('attn'), may hold values from -0.25 to 0.25
- moe_input: bfloat16 [512, 7168], P('expert', 'attn'), may hold values from -6 to 6
- routes: int32 [512, 8], P('expert'), may hold values from 0 to 15, all different within a row; in each aligned block of 32 rows (0 to 31, 32 to 63, ...) at most 32 rows name the same one
- route_scores: float32 [512, 8], P('expert'), may hold values from 0.05 to 1
- w_gate: bfloat16 [16, 7168, 2048], P('expert', None, 'attn'), may hold values from -0.0625 to 0.0625
- w_up: bfloat16 [16, 7168, 2048], P('expert', None, 'attn'), may hold values from -0.0625 to 0.0625
- w_down: bfloat16 [16, 2048, 7168], P('expert', 'attn'), may hold values from -0.125 to 0.125
Outputs:
- attn_values: bfloat16 [512, 8192], P('expert', 'attn')
- moe_out: bfloat16 [512, 7168], P('expert', 'attn')
Inputs may be any that keep to these rules, and one draw needn't show every extreme that they name: `lengths`: the longest prompt has exactly 256 valid positions. `routes`: each row names 8 different experts. Among the rows of one index of expert no expert is named by more than 32 rows, and in every draw some expert is named by exactly 32 of them.
All inputs are finite; a program needn't handle non-finite values.
Results may differ from a plain program's by a relative error of at most 0.012.
Values may be sent and summed in bfloat16 or wider, within the bound.
A program may use at most 128 MiB of HBM per device.

v0:
```python
from functools import partial

import jax
import jax.numpy as jnp
from jax import lax
from jax.sharding import PartitionSpec as P

score_scale = 192.0 ** (-0.5)
neg_fill = -1e30


def attend_prompt(query_block, prompt_keys, beam_keys, new_keys, length, latent_width):
    prompt_scores = (
        jnp.einsum("bhc,kc->bhk", query_block, prompt_keys, preferred_element_type=jnp.float32)
        * score_scale
    )
    positions = jnp.arange(prompt_keys.shape[0])
    prompt_scores = jnp.where(positions[None, None, :] < length, prompt_scores, neg_fill)
    beam_scores = (
        jnp.einsum("bhc,bgc->bhg", query_block, beam_keys, preferred_element_type=jnp.float32)
        * score_scale
    )
    new_scores = (
        jnp.einsum("bhc,bc->bh", query_block, new_keys, preferred_element_type=jnp.float32)
        * score_scale
    )
    top = jnp.maximum(
        jnp.maximum(jnp.max(prompt_scores, axis=-1), jnp.max(beam_scores, axis=-1)), new_scores
    )
    prompt_exp = jnp.exp(prompt_scores - top[..., None])
    beam_exp = jnp.exp(beam_scores - top[..., None])
    new_exp = jnp.exp(new_scores - top)
    total = jnp.sum(prompt_exp, axis=-1) + jnp.sum(beam_exp, axis=-1) + new_exp
    prompt_weight = (prompt_exp / total[..., None]).astype(jnp.bfloat16)
    beam_weight = (beam_exp / total[..., None]).astype(jnp.bfloat16)
    new_weight = (new_exp / total).astype(jnp.bfloat16)
    mixed = jnp.einsum(
        "bhk,kl->bhl",
        prompt_weight,
        prompt_keys[:, :latent_width],
        preferred_element_type=jnp.float32,
    )
    mixed = mixed + jnp.einsum(
        "bhg,bgl->bhl",
        beam_weight,
        beam_keys[:, :, :latent_width],
        preferred_element_type=jnp.float32,
    )
    mixed = mixed + new_weight.astype(jnp.float32)[..., None] * new_keys[
        :, None, :latent_width
    ].astype(jnp.float32)
    return mixed.astype(jnp.bfloat16)


def build_tables(routes, route_scores, experts, capacity):
    row_count, topk = routes.shape
    items = routes.reshape(-1)
    expert_hot = (items[:, None] == jnp.arange(experts)[None, :]).astype(jnp.int32)
    earlier = jnp.cumsum(expert_hot, axis=0) - expert_hot
    slot_index = jnp.sum(earlier * expert_hot, axis=1)
    target = items * capacity + slot_index
    place_hot = target[:, None] == jnp.arange(experts * capacity)[None, :]
    row_hot = (jnp.arange(row_count * topk) // topk)[:, None] == jnp.arange(row_count)[None, :]
    send_table = jnp.dot(
        place_hot.T.astype(jnp.bfloat16),
        row_hot.astype(jnp.bfloat16),
        preferred_element_type=jnp.float32,
    ).astype(jnp.bfloat16)
    share = 2.5 * route_scores / jnp.sum(route_scores, axis=1, keepdims=True)
    take_table = jnp.einsum(
        "ir,i,is->rs",
        row_hot.astype(jnp.float32),
        share.reshape(-1),
        place_hot.astype(jnp.float32),
        precision=lax.Precision.HIGHEST,
    )
    return (send_table, take_table)


def expert_block(received, w_gate, w_up, w_down):
    sources, slots, width = received.shape
    flat_rows = received.reshape(sources * slots, width)
    gate_act = jnp.dot(flat_rows, w_gate[0], preferred_element_type=jnp.float32)
    up_act = jnp.dot(flat_rows, w_up[0], preferred_element_type=jnp.float32)
    hidden = (jax.nn.silu(gate_act) * up_act).astype(jnp.bfloat16)
    partial_out = jnp.dot(hidden, w_down[0], preferred_element_type=jnp.float32).reshape(
        sources, slots, width
    )
    return lax.psum_scatter(
        partial_out.astype(jnp.bfloat16), "attn", scatter_dimension=2, tiled=True
    )


def local(
    queries,
    prompt_cache,
    beam_cache,
    new_latent,
    parents,
    lengths,
    up_values,
    moe_input,
    routes,
    route_scores,
    w_gate,
    w_up,
    w_down,
):
    row_count, head_count, key_width = queries.shape
    prompt_count = prompt_cache.shape[0]
    beam_count = row_count // prompt_count
    latent_width = up_values.shape[1]
    parent_rows = jnp.arange(row_count) // beam_count * beam_count + parents
    picked = jnp.take(beam_cache, parent_rows, axis=0)
    attend = partial(attend_prompt, latent_width=latent_width)
    latents = jax.vmap(attend)(
        queries.reshape(prompt_count, beam_count, head_count, key_width),
        prompt_cache,
        picked.reshape(prompt_count, beam_count, -1, key_width),
        new_latent.reshape(prompt_count, beam_count, key_width),
        lengths,
    )
    latents = latents.reshape(row_count, head_count, latent_width)
    attn_values = (
        jnp.einsum("rhl,hlv->rhv", latents, up_values, preferred_element_type=jnp.float32)
        .astype(jnp.bfloat16)
        .reshape(row_count, -1)
    )
    experts = lax.axis_size("expert")
    topk = routes.shape[1]
    capacity = min(row_count, 2 * row_count * topk // experts)
    send_table, take_table = build_tables(routes, route_scores, experts, capacity)
    full_input = lax.all_gather(moe_input, "attn", axis=1, tiled=True)
    outgoing = (
        jnp.dot(send_table, full_input, preferred_element_type=jnp.float32)
        .astype(jnp.bfloat16)
        .reshape(experts, capacity, -1)
    )
    handled = expert_block(
        lax.all_to_all(outgoing, "expert", split_axis=0, concat_axis=0, tiled=True),
        w_gate,
        w_up,
        w_down,
    )
    returned = lax.all_to_all(handled, "expert", split_axis=0, concat_axis=0, tiled=True)
    moe_out = jnp.dot(
        take_table,
        returned.reshape(experts * capacity, -1).astype(jnp.float32),
        precision=lax.Precision.HIGHEST,
    ).astype(jnp.bfloat16)
    return (attn_values, moe_out)


def solution(mesh):
    in_specs = (
        P("expert", "attn", None),
        P("expert", None, None),
        P("expert", None, None),
        P("expert", None),
        P("expert"),
        P("expert"),
        P("attn", None, None),
        P("expert", "attn"),
        P("expert", None),
        P("expert", None),
        P("expert", None, "attn"),
        P("expert", None, "attn"),
        P("expert", "attn", None),
    )
    out_specs = (P("expert", "attn"), P("expert", "attn"))
    return jax.shard_map(local, mesh=mesh, in_specs=in_specs, out_specs=out_specs, check_vma=False)
```

profile of v0, /device:TPU:13, one launch (start us, length us, event | category | flops | bytes accessed | tf_op | source)
XLA Modules:
  0.0 410.7 jit_solution(6998798548183443932)
XLA Ops:
  7.2 0.0 copy-start
  7.2 0.0 reduce-scatter.2.cloned.1.call-start
  7.2 0.9 copy.20
  8.1 0.1 eq.61
  8.2 0.1 reshape.111
  8.3 0.6 reduce-window.6
  8.9 0.2 slice_reduce_fusion
  9.1 0.1 fusion.40
  9.2 7.4 %all_gather.3 = bf16[32,7168]{1,0:T(8,128)(2,1)S(1)} all-gather(bf16[32,3584]{1,0:T(8,128)(2,1)} %param.20), channel_id=1, replica_groups=mesh['expert'=16,'attn'=2] {'attn'}, dimensions={1}, use_global_device_ids=true | all-gather | bytes 688128 | tf_op jit(solution)/shard_map/all_gather | solution.py:133
  16.5 4.7 %convolution_convert_fusion = bf16[512,7168]{1,0:T(8,128)(2,1)} fusion(bf16[32,7168]{1,0:T(8,128)(2,1)S(1)} %all_gather.3, s32[256]{0:T(256)S(1)} %get-tuple-element.11, s32[256]{0:T(256)S(1)} %get-tuple-element.10), kind=kOutput, calls=%fused_computation.8 | convolution fusion | flops 247095296 | bytes 7800832 | tf_op jit(solution)/shard_map/dot_general | solution.py:135
  21.2 0.0 copy-start.5
  21.2 167.3 %all_to_all.10 = bf16[16,32,7168]{2,1,0:T(8,128)(2,1)S(1)} all-to-all(bf16[16,32,7168]{2,1,0:T(8,128)(2,1)} %bitcast.80), channel_id=1, replica_groups=mesh['expert'=16,'attn'=2] {'expert'}, dimensions={0} | all-to-all | bytes 14680064 | tf_op jit(solution)/shard_map/all_to_all | solution.py:140
  188.6 0.0 copy-done.5
  188.6 7.9 %fusion.2 = f32[512,1024]{1,0:T(8,128)S(1)} fusion(bf16[512,7168]{1,0:T(8,128)(2,1)S(1)} %bitcast.81, bf16[1,7168,1024]{2,1,0:T(8,128)(2,1)S(1)} %copy-done.5), kind=kOutput, calls=%fused_computation.3 | convolution fusion | flops 7516192768 | bytes 24117248 | tf_op jit(solution)/shard_map/dot_general | solution.py:84
  196.5 11.4 %multiply_convert_fusion = bf16[512,1024]{1,0:T(8,128)(2,1)S(1)} fusion(f32[512,1024]{1,0:T(8,128)S(1)} %fusion.2, bf16[512,7168]{1,0:T(8,128)(2,1)S(1)} %bitcast.82, bf16[1,7168,1024]{2,1,0:T(8,128)(2,1)} %param.23), kind=kOutput, calls=%fused_computation.10 | convolution fusion | flops 7519338496 | bytes 25165824 | tf_op jit(solution)/shard_map/dot_general | solution.py:83
  207.8 15.0 %fusion.6 = bf16[16,32,7168]{2,1,0:T(8,128)(2,1)} fusion(bf16[16,32,1024]{2,1,0:T(8,128)(2,1)S(1)} %bitcast.90, bf16[1,1024,7168]{2,1,0:T(8,128)(2,1)} %param.25), kind=kOutput, calls=%fused_computation.7 | convolution fusion | flops 7519862784 | bytes 23068672 | tf_op jit(solution)/shard_map/dot_general | solution.py:86
  222.8 0.0 reduce-scatter.2.cloned.1.call-update
  222.9 0.0 copy-start.7
  222.9 0.0 copy-start.2
  222.9 0.0 copy-start.8
  222.9 88.7 %reduce-scatter.2.cloned.1.call-done = bf16[16,32,3584]{2,1,0:T(8,128)(2,1)} async-done(((bf16[16,32,7168]{2,1,0:T(8,128)(2,1)}), bf16[16,32,3584]{2,1,0:T(8,128)(2,1)}) %reduce-scatter.2.cloned.1.call-update) | async-done | bytes 3670032 | tf_op jit(solution)/shard_map/reduce_scatter | solution.py:89
  311.7 6.4 %all-to-all-start.1 = ((bf16[16,32,3584]{2,1,0:T(8,128)(2,1)}), bf16[16,32,3584]{2,1,0:T(8,128)(2,1)}, u32[]{:S(2)}, u32[]{:S(2)}) async-start(bf16[16,32,3584]{2,1,0:T(8,128)(2,1)} %reduce-scatter.2.cloned.1.call-done), calls=%async_computation.2 | async-start | bytes 7340032 | tf_op jit(solution)/shard_map/all_to_all | solution.py:145
  318.0 0.0 copy-done.7
  318.0 0.0 copy-start.3
  318.1 0.1 broadcast_in_dim.42
  318.1 0.0 copy-done.2
  318.2 0.7 gather_fusion
  318.8 0.0 copy-done.8
  318.8 0.1 iota_compare_fusion.10
  318.9 0.1 broadcast_select_fusion
  319.1 0.0 copy-done
  319.1 0.0 copy-start.6
  319.1 0.0 copy-done.3
  319.1 0.5 fusion.33
  319.6 0.6 fusion.47
  320.2 0.2 copy-done.6
  320.3 0.7 fusion.46
  321.0 0.1 fusion.30
  321.1 0.4 fusion.19
  321.6 0.0 copy-start.1
  321.6 0.8 fusion.15
  322.4 0.5 add_convert_fusion
  322.9 0.9 copy-done.1
  323.8 0.0 copy-start.4
  323.8 1.1 fusion.13
  324.8 0.7 copy.37
  325.6 0.0 copy-done.4
  325.6 0.1 copy.23
  325.7 0.1 reshape.113
  325.8 0.4 fusion.21
  326.2 73.1 %all-to-all-done.1 = bf16[16,32,3584]{2,1,0:T(8,128)(2,1)} async-done(((bf16[16,32,3584]{2,1,0:T(8,128)(2,1)}), bf16[16,32,3584]{2,1,0:T(8,128)(2,1)}, u32[]{:S(2)}, u32[]{:S(2)}) %all-to-all-start.1) | async-done | bytes 3670048 | tf_op jit(solution)/shard_map/all_to_all | solution.py:145
  399.3 4.6 %convolution_convert_fusion.1 = bf16[32,3584]{1,0:T(8,128)(2,1)} fusion(f32[32,512]{1,0:T(8,128)S(1)} %fusion.21, bf16[512,3584]{1,0:T(8,128)(2,1)} %bitcast.21), kind=kOutput, calls=%fused_computation.9 | convolution fusion | flops 704757760 | bytes 3964928 | tf_op jit(solution)/shard_map/dot_general | solution.py:146
  (11 shorter events, 0.1 us)
Async XLA Ops:
  7.2 311.9 %copy-start = (bf16[32,32,576]{2,1,0:T(8,128)(2,1)S(1)}, bf16[32,32,576]{2,1,0:T(8,128)(2,1)}, u32[]{:S(2)}) copy-start(bf16[32,32,576]{2,1,0:T(8,128)(2,1)} %param.13) | copy-start | bytes 3538948
  7.2 304.5 %reduce-scatter.2.cloned.1.call-start = ((), (), s32[]{:S(2)}) async-start(), calls=%async_computation.3 | async-start | bytes 11010048 | tf_op jit(solution)/shard_map/reduce_scatter | solution.py:89
  21.2 167.4 %copy-start.5 = (bf16[1,7168,1024]{2,1,0:T(8,128)(2,1)S(1)}, bf16[1,7168,1024]{2,1,0:T(8,128)(2,1)}, u32[]{:S(2)}) copy-start(bf16[1,7168,1024]{2,1,0:T(8,128)(2,1)} %param.24) | copy-start | bytes 44040196
  222.9 95.2 %copy-start.7 = (s32[32]{0:T(128)S(1)}, s32[32]{0:T(128)}, u32[]{:S(2)}) copy-start(s32[32]{0:T(128)} %param.17) | copy-start | bytes 388
  222.9 95.3 %copy-start.2 = (bf16[32,16,576]{2,1,0:T(8,128)(2,1)S(1)}, bf16[32,16,576]{2,1,0:T(8,128)(2,1)}, u32[]{:S(2)}) copy-start(bf16[32,16,576]{2,1,0:T(8,128)(2,1)} %param.15) | copy-start | bytes 1769476
  222.9 95.9 %copy-start.8 = (s32[4]{0:T(128)S(1)}, s32[4]{0:T(128)}, u32[]{:S(2)}) copy-start(s32[4]{0:T(128)} %param.18) | copy-start | bytes 52
  311.7 87.6 %all-to-all-start.1 = ((bf16[16,32,3584]{2,1,0:T(8,128)(2,1)}), bf16[16,32,3584]{2,1,0:T(8,128)(2,1)}, u32[]{:S(2)}, u32[]{:S(2)}) async-start(bf16[16,32,3584]{2,1,0:T(8,128)(2,1)} %reduce-scatter.2.cloned.1.call-done), calls=%async_computation.2 | async-start | bytes 7340032 | tf_op jit(solution)/shard_map/all_to_all | solution.py:145
  318.0 1.1 copy-start.3
  319.1 1.3 copy-start.6
  321.6 2.2 copy-start.1
  323.8 1.8 copy-start.4
Sparse Core Ops, SparseCore 0:
  223.0 88.6 reduce-scatter.1
where the time goes:
time: 411 us
  blocking collectives  175 us (43%)
  waiting for transfers between devices  162 us (39%)
  matrix products  48 us (12%)
  between operations  14.2 us (3%)
  starting transfers between devices  6.41 us (2%)
    all_to_all x1, blocking collectives, local(): lax.all_to_all(outgoing, 'expert', split_axis=0, concat_axis=0, tiled=True)  167 us
    reduce_scatter x1, waiting for transfers between devices, expert_block(): lax.psum_scatter(partial_out.astype(jnp.bfloat16), 'attn', scatter_dimens...  88.7 us
    all_to_all x1, waiting for transfers between devices, local(): lax.all_to_all(handled, 'expert', split_axis=0, concat_axis=0, tiled=True)  73.1 us
    dot_general x1, matrix products, expert_block(): jnp.dot(hidden, w_down[0], preferred_element_type=jnp.float32)  15 us
    dot_general x1, matrix products, expert_block(): gate_act = jnp.dot(flat_rows, w_gate[0], preferred_element_type=jnp.float32)  11.4 us
  transfers between devices with their start and end apart: 2, of which 2 were waited for; matrix products, arithmetic and copies ran while one was open for 2% of the time, Pallas kernels for 0%

commit v1 on v0

--- a/solution.py
+++ b/solution.py
@@ -52,43 +52,18 @@
     return mixed.astype(jnp.bfloat16)
 
 
-def build_tables(routes, route_scores, experts, capacity):
-    row_count, topk = routes.shape
-    items = routes.reshape(-1)
-    expert_hot = (items[:, None] == jnp.arange(experts)[None, :]).astype(jnp.int32)
-    earlier = jnp.cumsum(expert_hot, axis=0) - expert_hot
-    slot_index = jnp.sum(earlier * expert_hot, axis=1)
-    target = items * capacity + slot_index
-    place_hot = target[:, None] == jnp.arange(experts * capacity)[None, :]
-    row_hot = (jnp.arange(row_count * topk) // topk)[:, None] == jnp.arange(row_count)[None, :]
-    send_table = jnp.dot(
-        place_hot.T.astype(jnp.bfloat16),
-        row_hot.astype(jnp.bfloat16),
-        preferred_element_type=jnp.float32,
-    ).astype(jnp.bfloat16)
+def expert_shares(routes, route_scores, experts):
     share = 2.5 * route_scores / jnp.sum(route_scores, axis=1, keepdims=True)
-    take_table = jnp.einsum(
-        "ir,i,is->rs",
-        row_hot.astype(jnp.float32),
-        share.reshape(-1),
-        place_hot.astype(jnp.float32),
-        precision=lax.Precision.HIGHEST,
-    )
-    return (send_table, take_table)
+    hot = routes[:, :, None] == jnp.arange(experts)[None, None, :]
+    return jnp.sum(jnp.where(hot, share[:, :, None], 0.0), axis=1)
 
 
-def expert_block(received, w_gate, w_up, w_down):
-    sources, slots, width = received.shape
-    flat_rows = received.reshape(sources * slots, width)
-    gate_act = jnp.dot(flat_rows, w_gate[0], preferred_element_type=jnp.float32)
-    up_act = jnp.dot(flat_rows, w_up[0], preferred_element_type=jnp.float32)
+def expert_block(rows, row_share, w_gate, w_up, w_down):
+    gate_act = jnp.dot(rows, w_gate[0], preferred_element_type=jnp.float32)
+    up_act = jnp.dot(rows, w_up[0], preferred_element_type=jnp.float32)
     hidden = (jax.nn.silu(gate_act) * up_act).astype(jnp.bfloat16)
-    partial_out = jnp.dot(hidden, w_down[0], preferred_element_type=jnp.float32).reshape(
-        sources, slots, width
-    )
-    return lax.psum_scatter(
-        partial_out.astype(jnp.bfloat16), "attn", scatter_dimension=2, tiled=True
-    )
+    partial_out = jnp.dot(hidden, w_down[0], preferred_element_type=jnp.float32)
+    return (partial_out * row_share[:, None]).astype(jnp.bfloat16)
 
 
 def local(
@@ -127,27 +102,13 @@
         .reshape(row_count, -1)
     )
     experts = lax.axis_size("expert")
-    topk = routes.shape[1]
-    capacity = min(row_count, 2 * row_count * topk // experts)
-    send_table, take_table = build_tables(routes, route_scores, experts, capacity)
-    full_input = lax.all_gather(moe_input, "attn", axis=1, tiled=True)
-    outgoing = (
-        jnp.dot(send_table, full_input, preferred_element_type=jnp.float32)
-        .astype(jnp.bfloat16)
-        .reshape(experts, capacity, -1)
-    )
-    handled = expert_block(
-        lax.all_to_all(outgoing, "expert", split_axis=0, concat_axis=0, tiled=True),
-        w_gate,
-        w_up,
-        w_down,
-    )
-    returned = lax.all_to_all(handled, "expert", split_axis=0, concat_axis=0, tiled=True)
-    moe_out = jnp.dot(
-        take_table,
-        returned.reshape(experts * capacity, -1).astype(jnp.float32),
-        precision=lax.Precision.HIGHEST,
-    ).astype(jnp.bfloat16)
+    shares = lax.all_gather(expert_shares(routes, route_scores, experts), "expert", axis=0, tiled=True)
+    row_share = lax.dynamic_index_in_dim(shares, lax.axis_index("expert"), axis=1, keepdims=False)
+    rows = lax.all_gather(moe_input, "expert", axis=0, tiled=True)
+    rows = lax.all_gather(rows, "attn", axis=1, tiled=True)
+    scaled = expert_block(rows, row_share, w_gate, w_up, w_down)
+    halves = lax.psum_scatter(scaled, "attn", scatter_dimension=1, tiled=True)
+    moe_out = lax.psum_scatter(halves, "expert", scatter_dimension=0, tiled=True)
     return (attn_values, moe_out)
 
 

time: 411 us -> 359 us (0.87)
  the two profiles are of different devices: /device:TPU:13 before, /device:TPU:0 now
where the time goes in v1:
time: 359 us
  waiting for transfers between devices  280 us (78%)
  matrix products  40.8 us (11%)
  blocking collectives  19.8 us (6%)
  between operations  14.1 us (4%)
    reduce_scatter x1, waiting for transfers between devices, local(): halves = lax.psum_scatter(scaled, 'attn', scatter_dimension=1, tiled=True)  88.3 us
    all_gather x1, waiting for transfers between devices, local(): rows = lax.all_gather(rows, 'attn', axis=1, tiled=True)  72.7 us
    reduce_scatter x1, waiting for transfers between devices, local(): lax.psum_scatter(halves, 'expert', scatter_dimension=0, tiled=True)  65.9 us
    all_gather x1, waiting for transfers between devices, local(): rows = lax.all_gather(moe_input, 'expert', axis=0, tiled=True)  52.6 us
    all_gather x1, blocking collectives, local(): lax.all_gather(expert_shares(routes, route_scores, experts), 'expert', ax...  19.8 us
    dot_general x1, matrix products, expert_block(): gate_act = jnp.dot(rows, w_gate[0], preferred_element_type=jnp.float32)  13.6 us
    dot_general x1, matrix products, expert_block(): up_act = jnp.dot(rows, w_up[0], preferred_element_type=jnp.float32)  13.2 us
    dot_general x1, matrix products, expert_block(): partial_out = jnp.dot(hidden, w_down[0], preferred_element_type=jnp.float32)  9.92 us
  transfers between devices with their start and end apart: 4, of which 4 were waited for; matrix products, arithmetic and copies ran while one was open for 2% of the time, Pallas kernels for 0%

profile of v1, /device:TPU:0, one launch (start us, length us, event | category | flops | bytes accessed | tf_op | source)
XLA Modules:
  0.0 358.8 jit_solution(15779794130220997399)
XLA Ops:
  7.2 0.0 copy-start
  7.2 0.0 copy-start.4
  7.2 0.0 copy-start.5
  7.2 0.0 all-gather.4.cloned.1.call-start
  7.2 0.7 all-gather.4.cloned.1.call-update
  7.9 0.0 all-gather.6.cloned.1.call-start
  8.0 52.6 %all-gather.4.cloned.1.call-done = bf16[512,3584]{1,0:T(8,128)(2,1)} async-done(((bf16[32,3584]{1,0:T(8,128)(2,1)}), bf16[512,3584]{1,0:T(8,128)(2,1)}) %all-gather.4.cloned.1.call-update) | async-done | bytes 3670032 | tf_op jit(solution)/shard_map/all_gather | solution.py:107
  60.6 0.0 all-gather.6.cloned.1.call-update
  60.6 0.0 reduce-scatter.3.cloned.1.call-start
  60.6 0.0 copy-done.4
  60.7 0.0 copy-done.5
  60.7 19.8 %all-gather = f32[16,32,16]{1,2,0:T(8,128)S(1)} all-gather(f32[1,32,16]{1,2,0:T(8,128)S(1)} %bitcast.62), channel_id=1, replica_groups=mesh['expert'=16,'attn'=2] {'expert'}, dimensions={0}, use_global_device_ids=true | all-gather | bytes 34816 | tf_op jit(solution)/shard_map/all_gather | solution.py:105
  80.5 0.1 reshape.68
  80.7 72.7 %all-gather.6.cloned.1.call-done = bf16[512,7168]{1,0:T(8,128)(2,1)} async-done(((bf16[512,3584]{1,0:T(8,128)(2,1)}), bf16[512,7168]{1,0:T(8,128)(2,1)}) %all-gather.6.cloned.1.call-update) | async-done | bytes 7340048 | tf_op jit(solution)/shard_map/all_gather | solution.py:108
  153.4 0.0 slice-start
  153.4 0.0 slice-start.1
  153.4 13.2 %fusion.2 = f32[512,1024]{1,0:T(8,128)S(1)} fusion(bf16[512,7168]{1,0:T(8,128)(2,1)} %all-gather.6.cloned.1.call-done, bf16[1,7168,1024]{2,1,0:T(8,128)(2,1)} %param.24), kind=kOutput, calls=%fused_computation.3 | convolution fusion | flops 7516192768 | bytes 24117248 | tf_op jit(solution)/shard_map/dot_general | solution.py:63
  166.6 0.0 slice-start.2
  166.6 0.0 slice-start.3
  166.6 13.6 %multiply_convert_fusion.1 = bf16[512,1024]{1,0:T(8,128)(2,1)S(1)} fusion(f32[512,1024]{1,0:T(8,128)S(1)} %fusion.2, bf16[512,7168]{1,0:T(8,128)(2,1)} %all-gather.6.cloned.1.call-done, bf16[1,7168,1024]{2,1,0:T(8,128)(2,1)} %param.23), kind=kOutput, calls=%fused_computation.8 | convolution fusion | flops 7519338496 | bytes 25165824 | tf_op jit(solution)/shard_map/dot_general | solution.py:62
  180.2 0.0 slice-done
  180.2 0.0 slice-done.1
  180.2 0.0 slice-done.2
  180.2 0.0 slice-done.3
  180.2 9.9 %multiply_convert_fusion = bf16[512,7168]{1,0:T(8,128)(2,1)} fusion(bf16[512,1024]{1,0:T(8,128)(2,1)S(1)} %multiply_convert_fusion.1, bf16[1,1024,7168]{2,1,0:T(8,128)(2,1)S(1)} %bitcast.67, f32[512]{0:T(512)S(1)} %bitcast.65), kind=kOutput, calls=%fused_computation.7 | convolution fusion | flops 7523532800 | bytes 23070720 | tf_op jit(solution)/shard_map/dot_general | solution.py:65
  190.2 0.0 reduce-scatter.3.cloned.1.call-update
  190.2 0.0 copy-start.7
  190.2 0.0 copy-start.2
  190.2 0.2 reduce-scatter.5.cloned.1.call-start
  190.4 88.3 %reduce-scatter.3.cloned.1.call-done = bf16[512,3584]{1,0:T(8,128)(2,1)} async-done(((bf16[512,7168]{1,0:T(8,128)(2,1)}), bf16[512,3584]{1,0:T(8,128)(2,1)}) %reduce-scatter.3.cloned.1.call-update) | async-done | bytes 3670032 | tf_op jit(solution)/shard_map/reduce_scatter | solution.py:110
  278.8 0.0 copy-start.8
  278.8 0.0 reduce-scatter.5.cloned.1.call-update
  278.8 0.0 copy-done.7
  278.8 0.0 copy-start.3
  278.8 0.1 broadcast_in_dim.53
  278.9 0.0 copy-done.2
  278.9 0.7 gather_fusion
  279.6 0.0 copy-done.8
  279.6 0.1 iota_compare_fusion.1
  279.7 0.1 broadcast_select_fusion
  279.8 0.0 copy-done
  279.9 0.0 copy-start.6
  279.9 0.0 copy-done.3
  279.9 0.5 fusion.25
  280.4 0.6 fusion.31
  280.9 0.2 copy-done.6
  281.1 0.7 fusion.30
  281.8 0.1 fusion.22
  281.9 0.4 fusion.18
  282.3 0.0 copy-start.1
  282.3 0.8 fusion.14
  283.1 0.5 add_convert_fusion
  283.6 0.9 copy-done.1
  284.5 1.1 fusion.12
  285.6 0.7 copy.50
  286.3 65.9 %reduce-scatter.5.cloned.1.call-done = bf16[32,3584]{1,0:T(8,128)(2,1)} async-done(((bf16[512,3584]{1,0:T(8,128)(2,1)}), bf16[32,3584]{1,0:T(8,128)(2,1)}) %reduce-scatter.5.cloned.1.call-update) | async-done | bytes 229392 | tf_op jit(solution)/shard_map/reduce_scatter | solution.py:111
  (11 shorter events, 0.1 us)
Async XLA Ops:
  7.2 272.7 %copy-start = (bf16[32,32,576]{2,1,0:T(8,128)(2,1)S(1)}, bf16[32,32,576]{2,1,0:T(8,128)(2,1)}, u32[]{:S(2)}) copy-start(bf16[32,32,576]{2,1,0:T(8,128)(2,1)} %param.13) | copy-start | bytes 3538948
  7.2 53.4 %copy-start.4 = (f32[32,8]{0,1:T(8,128)S(1)}, f32[32,8]{0,1:T(8,128)}, u32[]{:S(2)}) copy-start(f32[32,8]{0,1:T(8,128)} %param.22) | copy-start | bytes 3076
  7.2 53.5 %copy-start.5 = (s32[32,8]{0,1:T(8,128)S(1)}, s32[32,8]{0,1:T(8,128)}, u32[]{:S(2)}) copy-start(s32[32,8]{0,1:T(8,128)} %param.21) | copy-start | bytes 3076
  7.2 53.4 %all-gather.4.cloned.1.call-start = ((), (), s32[]{:S(2)}) async-start(), calls=%async_computation.2 | async-start | bytes 3899392 | tf_op jit(solution)/shard_map/all_gather | solution.py:107
  7.9 145.4 %all-gather.6.cloned.1.call-start = ((), (), s32[]{:S(2)}) async-start(), calls=%async_computation.3 | async-start | bytes 11010048 | tf_op jit(solution)/shard_map/all_gather | solution.py:108
  60.6 218.2 %reduce-scatter.3.cloned.1.call-start = ((), (), s32[]{:S(2)}) async-start(), calls=%async_computation.4 | async-start | bytes 11010048 | tf_op jit(solution)/shard_map/reduce_scatter | solution.py:110
  153.4 26.8 %slice-start = ((s8[14680064]{0:T(1024)(128)(4,1)}), s8[4194304]{0:T(1024)(128)(4,1)S(1)}, s32[]{:S(2)}) async-start(s8[14680064]{0:T(1024)(128)(4,1)} %bitcast.66), calls=%async_computation.6 | async-start | bytes 8388608
  153.4 26.9 %slice-start.1 = ((s8[14680064]{0:T(1024)(128)(4,1)}), s8[4194304]{0:T(1024)(128)(4,1)S(1)}, s32[]{:S(2)}) async-start(s8[14680064]{0:T(1024)(128)(4,1)} %bitcast.66), calls=%async_computation.7 | async-start | bytes 8388608
  166.6 13.6 %slice-start.2 = ((s8[14680064]{0:T(1024)(128)(4,1)}), s8[4194304]{0:T(1024)(128)(4,1)S(1)}, s32[]{:S(2)}) async-start(s8[14680064]{0:T(1024)(128)(4,1)} %bitcast.66), calls=%async_computation.8 | async-start | bytes 8388608
  166.6 13.6 %slice-start.3 = ((s8[14680064]{0:T(1024)(128)(4,1)}), s8[2097152]{0:T(1024)(128)(4,1)S(1)}, s32[]{:S(2)}) async-start(s8[14680064]{0:T(1024)(128)(4,1)} %bitcast.66), calls=%async_computation.9 | async-start | bytes 4194304
  190.2 88.6 %copy-start.7 = (s32[32]{0:T(128)S(1)}, s32[32]{0:T(128)}, u32[]{:S(2)}) copy-start(s32[32]{0:T(128)} %param.17) | copy-start | bytes 388
  190.2 88.7 %copy-start.2 = (bf16[32,16,576]{2,1,0:T(8,128)(2,1)S(1)}, bf16[32,16,576]{2,1,0:T(8,128)(2,1)}, u32[]{:S(2)}) copy-start(bf16[32,16,576]{2,1,0:T(8,128)(2,1)} %param.15) | copy-start | bytes 1769476
  190.2 162.0 %reduce-scatter.5.cloned.1.call-start = ((), (), s32[]{:S(2)}) async-start(), calls=%async_computation.5 | async-start | bytes 3899392 | tf_op jit(solution)/shard_map/reduce_scatter | solution.py:111
  278.8 0.8 copy-start.8
  278.8 1.1 copy-start.3
  279.9 1.3 copy-start.6
  282.3 2.2 copy-start.1
Sparse Core Ops, SparseCore 0:
  10.3 50.1 all-gather.3
  62.1 91.2 all-gather.5
  190.3 88.4 reduce-scatter.2
  283.5 68.6 reduce-scatter.4

commit v2 on v1

--- a/solution.py
+++ b/solution.py
@@ -3,6 +3,8 @@
 import jax
 import jax.numpy as jnp
 from jax import lax
+from jax.experimental import pallas as pl
+from jax.experimental.pallas import tpu as pltpu
 from jax.sharding import PartitionSpec as P
 
 score_scale = 192.0 ** (-0.5)
@@ -64,6 +66,266 @@
     hidden = (jax.nn.silu(gate_act) * up_act).astype(jnp.bfloat16)
     partial_out = jnp.dot(hidden, w_down[0], preferred_element_type=jnp.float32)
     return (partial_out * row_share[:, None]).astype(jnp.bfloat16)
+
+
+class Links:
+    def __init__(self, send_sem, recv_sem):
+        expert = lax.axis_index("expert")
+        self.z, self.y, self.c = expert // 4, expert // 2 % 2, expert % 2
+        self.x = lax.axis_index("attn")
+        self.sems, self.count, self.copies = (send_sem, recv_sem), 0, []
+
+    def device(self, dz=0, fy=0, fc=0, fx=0):
+        return {"expert": self.expert_at(dz, fy, fc), "attn": self.flip(self.x, fx)}
+
+    def flip(self, value, by):
+        return 1 - value if by else value
+
+    def expert_at(self, dz=0, fy=0, fc=0):
+        return ((self.z + dz) % 4 * 2 + self.flip(self.y, fy)) * 2 + self.flip(self.c, fc)
+
+    def greet(self):
+        barrier = pltpu.get_barrier_semaphore()
+        others = [dict(fc=1), dict(fx=1), dict(fy=1), dict(dz=1), dict(dz=2), dict(dz=3)]
+        for other in others:
+            pl.semaphore_signal(
+                barrier, inc=1, device_id=self.device(**other), device_id_type=pl.DeviceIdType.MESH
+            )
+        pl.semaphore_wait(barrier, len(others))
+
+    def send(self, source, target, **other):
+        copy = pltpu.make_async_remote_copy(
+            src_ref=source,
+            dst_ref=target,
+            send_sem=self.sems[0].at[self.count],
+            recv_sem=self.sems[1].at[self.count],
+            device_id=self.device(**other),
+            device_id_type=pl.DeviceIdType.MESH,
+        )
+        self.count += 1
+        copy.start()
+        self.copies.append(copy)
+        return copy
+
+    def finish(self):
+        for copy in self.copies:
+            copy.wait_send()
+
+
+gather_copies = 62
+scatter_copies = 43
+
+
+def gather_kernel(x_ref, s_ref, out_ref, shares_ref, send_sem, recv_sem, local_sem):
+    rows, width = x_ref.shape
+    half = width // 2
+    links = Links(send_sem, recv_sem)
+
+    def block(d, fy=0, fx=0, h=None):
+        row = pl.multiple_of(links.expert_at(-d, fy) * rows, rows)
+        first = links.flip(links.x, fx) * width + (0 if h is None else h * half)
+        return out_ref.at[
+            pl.ds(row, rows), pl.ds(pl.multiple_of(first, 128), width if h is None else half)
+        ]
+
+    def share_block(d, fy=0):
+        return shares_ref.at[pl.ds(pl.multiple_of(links.expert_at(-d, fy) * rows, rows), rows)]
+
+    own = pltpu.make_async_copy(x_ref, block(0), local_sem.at[0])
+    own_share = pltpu.make_async_copy(s_ref, share_block(0), local_sem.at[1])
+    own.start()
+    own_share.start()
+    links.greet()
+    order = (0, 1, 3, 2)
+    by_z, by_z_share = {}, {}
+    by_x, by_y, by_xy, by_yx, by_y_share, last = {}, {}, {}, {}, {}, []
+
+    def source(d, h=None):
+        if d:
+            return block(d, h=h)
+        return x_ref if h is None else x_ref.at[:, pl.ds(h * half, half)]
+
+    def spread(d):
+        if d:
+            by_z[d].wait_recv()
+        by_x[d, 0] = links.send(source(d, 0), block(d, h=0), fx=1)
+        by_y[d, 1] = links.send(source(d, 1), block(d, h=1), fy=1)
+        by_x[d, 1] = links.send(source(d, 1), block(d, h=1), fx=1)
+        by_y[d, 0] = links.send(source(d, 0), block(d, h=0), fy=1)
+        last.append(links.send(source(d), block(d), fc=1))
+        if d:
+            by_z_share[d].wait_recv()
+        shares = share_block(d) if d else s_ref
+        by_y_share[d] = links.send(shares, share_block(d), fy=1)
+        last.append(links.send(shares, share_block(d), fc=1))
+
+    def relay(d):
+        by_x[d, 0].wait_recv()
+        by_xy[d] = links.send(block(d, fx=1, h=0), block(d, fx=1, h=0), fy=1)
+        by_y[d, 1].wait_recv()
+        by_yx[d] = links.send(block(d, fy=1, h=1), block(d, fy=1, h=1), fx=1)
+        by_x[d, 1].wait_recv()
+        last.append(links.send(block(d, fx=1), block(d, fx=1), fc=1))
+        by_y[d, 0].wait_recv()
+        last.append(links.send(block(d, fy=1), block(d, fy=1), fc=1))
+        by_y_share[d].wait_recv()
+        last.append(links.send(share_block(d, 1), share_block(d, 1), fc=1))
+
+    def settle(d):
+        by_xy[d].wait_recv()
+        last.append(links.send(block(d, 1, 1, 0), block(d, 1, 1, 0), fc=1))
+        by_yx[d].wait_recv()
+        last.append(links.send(block(d, 1, 1, 1), block(d, 1, 1, 1), fc=1))
+
+    for d in (1, 3, 2):
+        by_z[d] = links.send(x_ref, block(0), dz=d)
+        by_z_share[d] = links.send(s_ref, share_block(0), dz=d)
+    for step in range(6):
+        if step < 4:
+            spread(order[step])
+        if 0 <= step - 1 < 4:
+            relay(order[step - 1])
+        if step >= 2:
+            settle(order[step - 2])
+    for copy in last:
+        copy.wait_recv()
+    own.wait()
+    own_share.wait()
+    links.finish()
+
+
+def gather_rows(moe_input, shares):
+    rows, width = moe_input.shape
+    experts, groups = lax.axis_size("expert"), lax.axis_size("attn")
+    return pl.pallas_call(
+        gather_kernel,
+        out_shape=(
+            jax.ShapeDtypeStruct((experts * rows, groups * width), moe_input.dtype),
+            jax.ShapeDtypeStruct((experts * rows, shares.shape[1]), shares.dtype),
+        ),
+        in_specs=[pl.BlockSpec(memory_space=pl.ANY)] * 2,
+        out_specs=[pl.BlockSpec(memory_space=pl.ANY)] * 2,
+        scratch_shapes=[
+            pltpu.SemaphoreType.DMA((gather_copies,)),
+            pltpu.SemaphoreType.DMA((gather_copies,)),
+            pltpu.SemaphoreType.DMA((2,)),
+        ],
+        compiler_params=pltpu.CompilerParams(collective_id=0, has_side_effects=True),
+    )(moe_input, shares)
+
+
+def scatter_kernel(
+    p_ref, out_ref, sums, from_x, from_y, second_x, second_y, from_z, send_sem, recv_sem
+):
+    rows, width = out_ref.shape
+    half = width // 2
+    halves = (pl.ds(0, half), pl.ds(half, half))
+    links = Links(send_sem, recv_sem)
+    order = (1, 3, 2, 0)
+    pieces = ((1, 1), (1, 0), (0, 1), (0, 0))
+    by_core, by_x, by_y, by_x2, by_y2, by_z = {}, {}, {}, {}, {}, {}
+
+    def place(d, fx, fy, fc):
+        row = pl.multiple_of(links.expert_at(d, fy, fc) * rows, rows)
+        return row, links.flip(links.x, fx) * width
+
+    def wide(*refs):
+        total = refs[0].astype(jnp.float32)
+        for value in refs[1:]:
+            total = total + value.astype(jnp.float32)
+        return total.astype(jnp.bfloat16)
+
+    def add_core(d, fx, fy):
+        by_core[d, fx, fy].wait_recv()
+        row, column = place(d, fx, fy, 0)
+        for h in range(2):
+            first = pl.multiple_of(column + h * half, 128)
+            mine = p_ref[pl.ds(row, rows), pl.ds(first, half)]
+            sums[d, fx, fy, :, halves[h]] = wide(sums[d, fx, fy, :, halves[h]], mine)
+
+    def first_hop(d):
+        add_core(d, 1, 1)
+        by_x[d, 1] = links.send(sums.at[d, 1, 1, :, halves[0]], from_x.at[d, 1], fx=1)
+        by_y[d, 1] = links.send(sums.at[d, 1, 1, :, halves[1]], from_y.at[d, 1], fy=1)
+        add_core(d, 1, 0)
+        by_x[d, 0] = links.send(sums.at[d, 1, 0, :, halves[0]], from_x.at[d, 0], fx=1)
+        add_core(d, 0, 1)
+        by_y[d, 0] = links.send(sums.at[d, 0, 1, :, halves[1]], from_y.at[d, 0], fy=1)
+        add_core(d, 0, 0)
+
+    def second_hop(d):
+        by_x[d, 1].wait_recv()
+        sums[d, 0, 1, :, halves[0]] = wide(sums[d, 0, 1, :, halves[0]], from_x[d, 1])
+        by_y2[d] = links.send(sums.at[d, 0, 1, :, halves[0]], second_y.at[d], fy=1)
+        by_y[d, 1].wait_recv()
+        sums[d, 1, 0, :, halves[1]] = wide(sums[d, 1, 0, :, halves[1]], from_y[d, 1])
+        by_x2[d] = links.send(sums.at[d, 1, 0, :, halves[1]], second_x.at[d], fx=1)
+
+    def third_hop(d):
+        by_x[d, 0].wait_recv()
+        by_y2[d].wait_recv()
+        sums[d, 0, 0, :, halves[0]] = wide(
+            sums[d, 0, 0, :, halves[0]], from_x[d, 0], second_y[d]
+        )
+        by_y[d, 0].wait_recv()
+        by_x2[d].wait_recv()
+        sums[d, 0, 0, :, halves[1]] = wide(
+            sums[d, 0, 0, :, halves[1]], from_y[d, 0], second_x[d]
+        )
+        if d:
+            by_z[d] = links.send(sums.at[d, 0, 0], from_z.at[d - 1], dz=d)
+
+    links.greet()
+    for d in order:
+        for fx, fy in pieces:
+            row, column = place(d, fx, fy, 1)
+            by_core[d, fx, fy] = links.send(
+                p_ref.at[pl.ds(row, rows), pl.ds(pl.multiple_of(column, 128), width)],
+                sums.at[d, fx, fy],
+                fc=1,
+            )
+    for step in range(6):
+        if step < 4:
+            first_hop(order[step])
+        if 0 <= step - 1 < 4:
+            second_hop(order[step - 1])
+        if step >= 2:
+            third_hop(order[step - 2])
+    for d in (1, 3, 2):
+        by_z[d].wait_recv()
+    for h in range(2):
+        out_ref[:, halves[h]] = wide(
+            sums[0, 0, 0, :, halves[h]],
+            from_z[0, :, halves[h]],
+            from_z[1, :, halves[h]],
+            from_z[2, :, halves[h]],
+        )
+    links.finish()
+
+
+def scatter_rows(scaled):
+    rows = scaled.shape[0] // lax.axis_size("expert")
+    width = scaled.shape[1] // lax.axis_size("attn")
+    kind = scaled.dtype
+    return pl.pallas_call(
+        scatter_kernel,
+        out_shape=jax.ShapeDtypeStruct((rows, width), kind),
+        in_specs=[pl.BlockSpec(memory_space=pltpu.VMEM)],
+        out_specs=pl.BlockSpec(memory_space=pltpu.VMEM),
+        scratch_shapes=[
+            pltpu.VMEM((4, 2, 2, rows, width), kind),
+            pltpu.VMEM((4, 2, rows, width // 2), kind),
+            pltpu.VMEM((4, 2, rows, width // 2), kind),
+            pltpu.VMEM((4, rows, width // 2), kind),
+            pltpu.VMEM((4, rows, width // 2), kind),
+            pltpu.VMEM((3, rows, width), kind),
+            pltpu.SemaphoreType.DMA((scatter_copies,)),
+            pltpu.SemaphoreType.DMA((scatter_copies,)),
+        ],
+        compiler_params=pltpu.CompilerParams(
+            collective_id=1, has_side_effects=True, vmem_limit_bytes=40 * 1024 * 1024
+        ),
+    )(scaled)
 
 
 def local(
@@ -102,13 +364,22 @@
         .reshape(row_count, -1)
     )
     experts = lax.axis_size("expert")
-    shares = lax.all_gather(expert_shares(routes, route_scores, experts), "expert", axis=0, tiled=True)
+    own_shares = expert_shares(routes, route_scores, experts)
+    on_grid = experts == 16 and lax.axis_size("attn") == 2
+    if on_grid:
+        own_shares = jnp.pad(own_shares, ((0, 0), (0, 128 - experts)))
+        rows, shares = gather_rows(moe_input, own_shares)
+    else:
+        shares = lax.all_gather(own_shares, "expert", axis=0, tiled=True)
+        rows = lax.all_gather(moe_input, "expert", axis=0, tiled=True)
+        rows = lax.all_gather(rows, "attn", axis=1, tiled=True)
     row_share = lax.dynamic_index_in_dim(shares, lax.axis_index("expert"), axis=1, keepdims=False)
-    rows = lax.all_gather(moe_input, "expert", axis=0, tiled=True)
-    rows = lax.all_gather(rows, "attn", axis=1, tiled=True)
     scaled = expert_block(rows, row_share, w_gate, w_up, w_down)
-    halves = lax.psum_scatter(scaled, "attn", scatter_dimension=1, tiled=True)
-    moe_out = lax.psum_scatter(halves, "expert", scatter_dimension=0, tiled=True)
+    if on_grid:
+        moe_out = scatter_rows(scaled)
+    else:
+        halves = lax.psum_scatter(scaled, "attn", scatter_dimension=1, tiled=True)
+        moe_out = lax.psum_scatter(halves, "expert", scatter_dimension=0, tiled=True)
     return (attn_values, moe_out)
 
 

time: 359 us -> 140 us (0.39)
  waiting for transfers between devices: 280 us -> 0 us
  Pallas kernels: 0 us -> 87.6 us
  blocking collectives: 19.8 us -> 0 us
  between operations: 14.1 us -> 0.88 us
  other arithmetic: 0.77 us -> 4.92 us
  local copies, waits for them, and re-layouts: 2.8 us -> 6.85 us
    reduce_scatter x2 -> x0, waiting for transfers between devices: 154 us -> none  [the longest x1 88.3 us: local(): halves = lax.psum_scatter(scaled, 'attn', scatter_dimension=1, tiled=True)]
    all_gather x2 -> x0, waiting for transfers between devices: 125 us -> none  [the longest x1 72.7 us: local(): rows = lax.all_gather(rows, 'attn', axis=1, tiled=True)]
    pallas_call x0 -> x2, Pallas kernels: none -> 87.6 us  [the longest x1 45.5 us: scatter_rows(): pl.pallas_call(scatter_kernel, out_shape=jax.ShapeDtypeStruct((rows, widt...]
    all_gather x1 -> x0, blocking collectives: 19.8 us -> none  [local(): lax.all_gather(expert_shares(routes, route_scores, experts), 'expert', ax...]
    dot_general x1, matrix products: 13.6 us -> 7.97 us  [expert_block(): gate_act = jnp.dot(rows, w_gate[0], preferred_element_type=jnp.float32)]
  transfers between devices with their start and end apart: 4 -> 0, of which waited for: 4 -> 0; matrix products, arithmetic and copies ran while one was open for 2% -> 0% of each run, Pallas kernels for 0% -> 0%
where the time goes in v2:
time: 140 us
  Pallas kernels  87.6 us (63%)
  matrix products  39.4 us (28%)
  local copies, waits for them, and re-layouts  6.85 us (5%)
  other arithmetic  4.92 us (4%)
    pallas_call x1, Pallas kernels, scatter_rows(): pl.pallas_call(scatter_kernel, out_shape=jax.ShapeDtypeStruct((rows, widt...  45.5 us
    pallas_call x1, Pallas kernels, gather_rows(): pl.pallas_call(gather_kernel, out_shape=(jax.ShapeDtypeStruct((experts *...  42.1 us
    dot_general x1, matrix products, expert_block(): partial_out = jnp.dot(hidden, w_down[0], preferred_element_type=jnp.float32)  13.4 us
    dot_general x1, matrix products, expert_block(): up_act = jnp.dot(rows, w_up[0], preferred_element_type=jnp.float32)  13.2 us
    dot_general x1, matrix products, expert_block(): gate_act = jnp.dot(rows, w_gate[0], preferred_element_type=jnp.float32)  7.97 us
    unnamed x21, local copies, waits for them, and re-layouts  3.46 us

profile of v2, /device:TPU:0, one launch (start us, length us, event | category | flops | bytes accessed | tf_op | source)
XLA Modules:
  0.0 139.7 jit_solution(12196054388408820867)
XLA Ops:
  0.6 0.0 copy-start
  0.6 0.0 copy-start.3
  0.7 1.3 copy-done
  2.0 0.7 reduce_sum.38
  2.7 0.7 iota_compare_fusion.1
  3.4 0.7 compare_and_fusion
  4.1 0.1 broadcast_in_dim.53
  4.1 0.7 multiply_divide_fusion
  4.8 0.7 select_reduce_fusion
  5.6 0.1 copy.27
  5.6 0.6 pad.4.s_ref
  6.2 1.3 fusion.25
  7.5 0.8 slice_convert_fusion
  8.3 0.0 copy-done.3
  8.3 0.7 gather_fusion
  9.0 0.0 copy-start.5
  9.0 0.1 broadcast_select_fusion
  9.1 0.5 fusion.31
  9.7 0.6 copy-done.5
  10.2 0.7 fusion.30
  10.9 0.1 fusion.22
  11.0 0.4 fusion.18
  11.4 0.0 copy-start.2
  11.5 0.8 fusion.14
  12.2 0.5 add_convert_fusion
  12.8 0.9 copy-done.2
  13.6 1.1 fusion.12
  14.7 0.0 slice-start
  14.7 0.7 copy.39
  15.5 42.1 %shard_map.140 = (bf16[512,7168]{1,0:T(8,128)(2,1)}, f32[512,128]{1,0:T(8,128)}) custom-call(bf16[32,3584]{1,0:T(8,128)(2,1)} %x_ref.1, f32[32,128]{1,0:T(8,128)} %pad.4.s_ref), custom_call_target="tpu_custom_call" | custom-call | tf_op jit(solution)/shard_map/pallas_call | solution.py:200
  57.6 1.2 dynamic-slice_reduce_fusion
  58.8 0.0 slice-start.1
  58.8 0.0 slice-start.2
  58.8 0.0 slice-start.3
  58.8 0.0 copy-start.4
  58.8 13.2 %fusion.2 = f32[512,1024]{1,0:T(8,128)S(1)} fusion(bf16[512,7168]{1,0:T(8,128)(2,1)} %get-tuple-element.4, bf16[1,7168,1024]{2,1,0:T(8,128)(2,1)} %param.24), kind=kOutput, calls=%fused_computation.3 | convolution fusion | flops 7516192768 | bytes 24117248 | tf_op jit(solution)/shard_map/dot_general | solution.py:65
  72.1 0.0 slice-done
  72.1 0.0 slice-done.1
  72.1 0.0 slice-done.2
  72.1 0.0 slice-done.3
  72.1 0.0 copy-done.4
  72.1 8.0 %multiply_convert_fusion.1 = bf16[512,1024]{1,0:T(8,128)(2,1)S(1)} fusion(f32[512,1024]{1,0:T(8,128)S(1)} %fusion.2, bf16[512,7168]{1,0:T(8,128)(2,1)S(1)} %copy-done.4, bf16[1,7168,1024]{2,1,0:T(8,128)(2,1)S(1)} %bitcast.61), kind=kOutput, calls=%fused_computation.8 | convolution fusion | flops 7519338496 | bytes 25165824 | tf_op jit(solution)/shard_map/dot_general | solution.py:64
  80.1 13.4 %multiply_convert_fusion.p_ref = bf16[512,7168]{1,0:T(8,128)(2,1)S(1)} fusion(bf16[512,1024]{1,0:T(8,128)(2,1)S(1)} %multiply_convert_fusion.1, bf16[1,1024,7168]{2,1,0:T(8,128)(2,1)} %param.25, f32[512]{0:T(512)S(1)} %dynamic-slice_reduce_fusion), kind=kOutput, calls=%fused_computation.7 | convolution fusion | flops 7523532800 | bytes 23070720 | tf_op jit(solution)/shard_map/dot_general | solution.py:67
  93.5 0.0 copy-start.1
  93.5 45.5 %shard_map.141 = bf16[32,3584]{1,0:T(8,128)(2,1)S(1)} custom-call(bf16[512,7168]{1,0:T(8,128)(2,1)S(1)} %multiply_convert_fusion.p_ref), custom_call_target="tpu_custom_call" | custom-call | tf_op jit(solution)/shard_map/pallas_call | solution.py:310
  139.0 0.7 copy.41
  139.7 0.0 copy-done.1
  (4 shorter events, 0.0 us)
Async XLA Ops:
  0.6 1.3 copy-start
  0.6 7.7 %copy-start.3 = (bf16[32,16,576]{2,1,0:T(8,128)(2,1)S(1)}, bf16[32,16,576]{2,1,0:T(8,128)(2,1)}, u32[]{:S(2)}) copy-start(bf16[32,16,576]{2,1,0:T(8,128)(2,1)} %param.15) | copy-start | bytes 1769476
  9.0 1.3 copy-start.5
  11.4 2.2 %copy-start.2 = (bf16[32,512,128]{2,1,0:T(8,128)(2,1)S(1)}, bf16[32,512,128]{2,1,0:T(8,128)(2,1)}, u32[]{:S(2)}) copy-start(bf16[32,512,128]{2,1,0:T(8,128)(2,1)} %param.19) | copy-start | bytes 12582916
  14.7 57.4 %slice-start = ((s8[14680064]{0:T(1024)(128)(4,1)}), s8[2097152]{0:T(1024)(128)(4,1)S(1)}, s32[]{:S(2)}) async-start(s8[14680064]{0:T(1024)(128)(4,1)} %bitcast.60), calls=%async_computation | async-start | bytes 4194304
  58.8 13.3 %slice-start.1 = ((s8[14680064]{0:T(1024)(128)(4,1)}), s8[4194304]{0:T(1024)(128)(4,1)S(1)}, s32[]{:S(2)}) async-start(s8[14680064]{0:T(1024)(128)(4,1)} %bitcast.60), calls=%async_computation.1 | async-start | bytes 8388608
  58.8 13.3 %slice-start.2 = ((s8[14680064]{0:T(1024)(128)(4,1)}), s8[4194304]{0:T(1024)(128)(4,1)S(1)}, s32[]{:S(2)}) async-start(s8[14680064]{0:T(1024)(128)(4,1)} %bitcast.60), calls=%async_computation.2 | async-start | bytes 8388608
  58.8 13.3 %slice-start.3 = ((s8[14680064]{0:T(1024)(128)(4,1)}), s8[4194304]{0:T(1024)(128)(4,1)S(1)}, s32[]{:S(2)}) async-start(s8[14680064]{0:T(1024)(128)(4,1)} %bitcast.60), calls=%async_computation.3 | async-start | bytes 8388608
  58.8 13.3 %copy-start.4 = (bf16[512,7168]{1,0:T(8,128)(2,1)S(1)}, bf16[512,7168]{1,0:T(8,128)(2,1)}, u32[]{:S(2)}) copy-start(bf16[512,7168]{1,0:T(8,128)(2,1)} %get-tuple-element.4) | copy-start | bytes 22020100
  93.5 46.2 %copy-start.1 = (bf16[32,32,576]{2,1,0:T(8,128)(2,1)S(1)}, bf16[32,32,576]{2,1,0:T(8,128)(2,1)}, u32[]{:S(2)}) copy-start(bf16[32,32,576]{2,1,0:T(8,128)(2,1)} %param.13) | copy-start | bytes 3538948

commit v3 on v2

--- a/solution.py
+++ b/solution.py
@@ -82,7 +82,7 @@
         return 1 - value if by else value
 
     def expert_at(self, dz=0, fy=0, fc=0):
-        return ((self.z + dz) % 4 * 2 + self.flip(self.y, fy)) * 2 + self.flip(self.c, fc)
+        return ((self.z + dz + 4) % 4 * 2 + self.flip(self.y, fy)) * 2 + self.flip(self.c, fc)
 
     def greet(self):
         barrier = pltpu.get_barrier_semaphore()
@@ -116,7 +116,10 @@
 scatter_copies = 43
 
 
-def gather_kernel(x_ref, s_ref, out_ref, shares_ref, send_sem, recv_sem, local_sem):
+def gather_kernel(
+    experts, x_ref, routes_ref, scores_ref, gate_ref, up_ref, hidden_ref, shares_ref,
+    out_ref, gate_held, up_held, send_sem, recv_sem, local_sem
+):
     rows, width = x_ref.shape
     half = width // 2
     links = Links(send_sem, recv_sem)
@@ -132,13 +135,23 @@
         return shares_ref.at[pl.ds(pl.multiple_of(links.expert_at(-d, fy) * rows, rows), rows)]
 
     own = pltpu.make_async_copy(x_ref, block(0), local_sem.at[0])
-    own_share = pltpu.make_async_copy(s_ref, share_block(0), local_sem.at[1])
+    gate_copy = pltpu.make_async_copy(gate_ref.at[0], gate_held, local_sem.at[1])
+    up_copy = pltpu.make_async_copy(up_ref.at[0], up_held, local_sem.at[2])
     own.start()
-    own_share.start()
+    gate_copy.start()
+    up_copy.start()
+    lanes = lax.broadcasted_iota(jnp.int32, (rows, shares_ref.shape[1]), 1)
+    scores = scores_ref[...]
+    share = 2.5 * scores / jnp.sum(scores, axis=1, keepdims=True)
+    own_share = jnp.zeros(lanes.shape, jnp.float32)
+    for k in range(scores.shape[1]):
+        own_share = own_share + jnp.where(lanes == routes_ref[:, k : k + 1], share[:, k : k + 1], 0.0)
+    shares_ref[pl.ds(pl.multiple_of(links.expert_at() * rows, rows), rows), :] = own_share
     links.greet()
     order = (0, 1, 3, 2)
     by_z, by_z_share = {}, {}
-    by_x, by_y, by_xy, by_yx, by_y_share, last = {}, {}, {}, {}, {}, []
+    by_x, by_y, by_xy, by_yx, by_y_share = {}, {}, {}, {}, {}
+    last = {d: [] for d in order}
 
     def source(d, h=None):
         if d:
@@ -152,12 +165,12 @@
         by_y[d, 1] = links.send(source(d, 1), block(d, h=1), fy=1)
         by_x[d, 1] = links.send(source(d, 1), block(d, h=1), fx=1)
         by_y[d, 0] = links.send(source(d, 0), block(d, h=0), fy=1)
-        last.append(links.send(source(d), block(d), fc=1))
+        last[d].append(links.send(source(d), block(d), fc=1))
         if d:
             by_z_share[d].wait_recv()
-        shares = share_block(d) if d else s_ref
+        shares = share_block(d)
         by_y_share[d] = links.send(shares, share_block(d), fy=1)
-        last.append(links.send(shares, share_block(d), fc=1))
+        last[d].append(links.send(shares, share_block(d), fc=1))
 
     def relay(d):
         by_x[d, 0].wait_recv()
@@ -165,57 +178,80 @@
         by_y[d, 1].wait_recv()
         by_yx[d] = links.send(block(d, fy=1, h=1), block(d, fy=1, h=1), fx=1)
         by_x[d, 1].wait_recv()
-        last.append(links.send(block(d, fx=1), block(d, fx=1), fc=1))
+        last[d].append(links.send(block(d, fx=1), block(d, fx=1), fc=1))
         by_y[d, 0].wait_recv()
-        last.append(links.send(block(d, fy=1), block(d, fy=1), fc=1))
+        last[d].append(links.send(block(d, fy=1), block(d, fy=1), fc=1))
         by_y_share[d].wait_recv()
-        last.append(links.send(share_block(d, 1), share_block(d, 1), fc=1))
+        last[d].append(links.send(share_block(d, 1), share_block(d, 1), fc=1))
 
     def settle(d):
         by_xy[d].wait_recv()
-        last.append(links.send(block(d, 1, 1, 0), block(d, 1, 1, 0), fc=1))
+        last[d].append(links.send(block(d, 1, 1, 0), block(d, 1, 1, 0), fc=1))
         by_yx[d].wait_recv()
-        last.append(links.send(block(d, 1, 1, 1), block(d, 1, 1, 1), fc=1))
+        last[d].append(links.send(block(d, 1, 1, 1), block(d, 1, 1, 1), fc=1))
+
+    def compute(d):
+        if d == 0:
+            own.wait()
+            gate_copy.wait()
+            up_copy.wait()
+        for copy in last[d]:
+            copy.wait_recv()
+        group = pl.ds(pl.multiple_of((links.z - d + 4) % 4 * (4 * rows), 4 * rows), 4 * rows)
+
+        @pl.loop(0, hidden_ref.shape[1] // 256)
+        def _(tile):
+            columns = pl.ds(pl.multiple_of(tile * 256, 256), 256)
+            gate = jnp.dot(out_ref[group, :], gate_held[:, columns], preferred_element_type=jnp.float32)
+            up = jnp.dot(out_ref[group, :], up_held[:, columns], preferred_element_type=jnp.float32)
+            hidden_ref[group, columns] = (jax.nn.silu(gate) * up).astype(hidden_ref.dtype)
 
     for d in (1, 3, 2):
         by_z[d] = links.send(x_ref, block(0), dz=d)
-        by_z_share[d] = links.send(s_ref, share_block(0), dz=d)
+        by_z_share[d] = links.send(share_block(0), share_block(0), dz=d)
     for step in range(6):
         if step < 4:
             spread(order[step])
         if 0 <= step - 1 < 4:
             relay(order[step - 1])
+        if step >= 3:
+            compute(order[step - 3])
         if step >= 2:
             settle(order[step - 2])
-    for copy in last:
-        copy.wait_recv()
-    own.wait()
-    own_share.wait()
+    compute(order[3])
     links.finish()
 
 
-def gather_rows(moe_input, shares):
+def gather_rows(moe_input, routes, route_scores, w_gate, w_up):
     rows, width = moe_input.shape
     experts, groups = lax.axis_size("expert"), lax.axis_size("attn")
+    kind, units = moe_input.dtype, w_gate.shape[2]
     return pl.pallas_call(
-        gather_kernel,
+        partial(gather_kernel, experts),
         out_shape=(
-            jax.ShapeDtypeStruct((experts * rows, groups * width), moe_input.dtype),
-            jax.ShapeDtypeStruct((experts * rows, shares.shape[1]), shares.dtype),
+            jax.ShapeDtypeStruct((experts * rows, units), kind),
+            jax.ShapeDtypeStruct((experts * rows, 128), jnp.float32),
         ),
-        in_specs=[pl.BlockSpec(memory_space=pl.ANY)] * 2,
-        out_specs=[pl.BlockSpec(memory_space=pl.ANY)] * 2,
+        in_specs=[pl.BlockSpec(memory_space=pltpu.VMEM)] * 3
+        + [pl.BlockSpec(memory_space=pl.ANY)] * 2,
+        out_specs=[pl.BlockSpec(memory_space=pltpu.VMEM)] * 2,
         scratch_shapes=[
+            pltpu.VMEM((experts * rows, groups * width), kind),
+            pltpu.VMEM(w_gate.shape[1:], kind),
+            pltpu.VMEM(w_up.shape[1:], kind),
             pltpu.SemaphoreType.DMA((gather_copies,)),
             pltpu.SemaphoreType.DMA((gather_copies,)),
-            pltpu.SemaphoreType.DMA((2,)),
+            pltpu.SemaphoreType.DMA((3,)),
         ],
-        compiler_params=pltpu.CompilerParams(collective_id=0, has_side_effects=True),
-    )(moe_input, shares)
+        compiler_params=pltpu.CompilerParams(
+            collective_id=0, has_side_effects=True, vmem_limit_bytes=54 * 1024 * 1024
+        ),
+    )(moe_input, routes, route_scores, w_gate, w_up)
 
 
 def scatter_kernel(
-    p_ref, out_ref, sums, from_x, from_y, second_x, second_y, from_z, send_sem, recv_sem
+    hidden_ref, shares_ref, down_ref, out_ref, p_ref, down_held,
+    sums, from_x, from_y, second_x, second_y, from_z, send_sem, recv_sem, local_sem
 ):
     rows, width = out_ref.shape
     half = width // 2
@@ -275,8 +311,33 @@
         if d:
             by_z[d] = links.send(sums.at[d, 0, 0], from_z.at[d - 1], dz=d)
 
-    links.greet()
-    for d in order:
+    parts = [pl.ds(part * half, half) for part in range(4)]
+    loads = [
+        pltpu.make_async_copy(
+            down_ref.at[0, :, parts[part]], down_held.at[:, parts[part]], local_sem.at[part]
+        )
+        for part in range(4)
+    ]
+
+    def produce(d):
+        group = pl.ds(pl.multiple_of((links.z + d) % 4 * (4 * rows), 4 * rows), 4 * rows)
+        shares = shares_ref[group, :]
+        lanes = lax.broadcasted_iota(jnp.int32, shares.shape, 1)
+        share = jnp.sum(
+            jnp.where(lanes == lax.axis_index("expert"), shares, 0.0), axis=1, keepdims=True
+        )
+        for part in range(4):
+            if d == order[0]:
+                loads[part].wait()
+
+            @pl.loop(0, half // 256)
+            def _(tile):
+                columns = pl.ds(pl.multiple_of(part * half + tile * 256, 256), 256)
+                product = jnp.dot(
+                    hidden_ref[group, :], down_held[:, columns], preferred_element_type=jnp.float32
+                )
+                p_ref[group, columns] = (product * share).astype(p_ref.dtype)
+
         for fx, fy in pieces:
             row, column = place(d, fx, fy, 1)
             by_core[d, fx, fy] = links.send(
@@ -284,7 +345,14 @@
                 sums.at[d, fx, fy],
                 fc=1,
             )
+
+    for load in loads:
+        load.start()
+    links.greet()
+    produce(order[0])
     for step in range(6):
+        if step + 1 < 4:
+            produce(order[step + 1])
         if step < 4:
             first_hop(order[step])
         if 0 <= step - 1 < 4:
@@ -303,16 +371,22 @@
     links.finish()
 
 
-def scatter_rows(scaled):
-    rows = scaled.shape[0] // lax.axis_size("expert")
-    width = scaled.shape[1] // lax.axis_size("attn")
-    kind = scaled.dtype
+def scatter_rows(hidden, shares, w_down):
+    count, full = hidden.shape[0], w_down.shape[2]
+    rows, width = count // lax.axis_size("expert"), full // lax.axis_size("attn")
+    kind = hidden.dtype
     return pl.pallas_call(
         scatter_kernel,
         out_shape=jax.ShapeDtypeStruct((rows, width), kind),
-        in_specs=[pl.BlockSpec(memory_space=pltpu.VMEM)],
+        in_specs=[
+            pl.BlockSpec(memory_space=pltpu.VMEM),
+            pl.BlockSpec(memory_space=pltpu.VMEM),
+            pl.BlockSpec(memory_space=pl.ANY),
+        ],
         out_specs=pl.BlockSpec(memory_space=pltpu.VMEM),
         scratch_shapes=[
+            pltpu.VMEM((count, full), kind),
+            pltpu.VMEM(w_down.shape[1:], kind),
             pltpu.VMEM((4, 2, 2, rows, width), kind),
             pltpu.VMEM((4, 2, rows, width // 2), kind),
             pltpu.VMEM((4, 2, rows, width // 2), kind),
@@ -321,11 +395,12 @@
             pltpu.VMEM((3, rows, width), kind),
             pltpu.SemaphoreType.DMA((scatter_copies,)),
             pltpu.SemaphoreType.DMA((scatter_copies,)),
+            pltpu.SemaphoreType.DMA((4,)),
         ],
         compiler_params=pltpu.CompilerParams(
-            collective_id=1, has_side_effects=True, vmem_limit_bytes=40 * 1024 * 1024
+            collective_id=1, has_side_effects=True, vmem_limit_bytes=48 * 1024 * 1024
         ),
-    )(scaled)
+    )(hidden, shares, w_down)
 
 
 def local(
@@ -364,20 +439,18 @@
         .reshape(row_count, -1)
     )
     experts = lax.axis_size("expert")
-    own_shares = expert_shares(routes, route_scores, experts)
-    on_grid = experts == 16 and lax.axis_size("attn") == 2
-    if on_grid:
-        own_shares = jnp.pad(own_shares, ((0, 0), (0, 128 - experts)))
-        rows, shares = gather_rows(moe_input, own_shares)
+    if experts == 16 and lax.axis_size("attn") == 2:
+        hidden, shares = gather_rows(moe_input, routes, route_scores, w_gate, w_up)
+        moe_out = scatter_rows(hidden, shares, w_down)
     else:
+        own_shares = expert_shares(routes, route_scores, experts)
         shares = lax.all_gather(own_shares, "expert", axis=0, tiled=True)
         rows = lax.all_gather(moe_input, "expert", axis=0, tiled=True)
         rows = lax.all_gather(rows, "attn", axis=1, tiled=True)
-    row_share = lax.dynamic_index_in_dim(shares, lax.axis_index("expert"), axis=1, keepdims=False)
-    scaled = expert_block(rows, row_share, w_gate, w_up, w_down)
-    if on_grid:
-        moe_out = scatter_rows(scaled)
-    else:
+        row_share = lax.dynamic_index_in_dim(
+            shares, lax.axis_index("expert"), axis=1, keepdims=False
+        )
+        scaled = expert_block(rows, row_share, w_gate, w_up, w_down)
         halves = lax.psum_scatter(scaled, "attn", scatter_dimension=1, tiled=True)
         moe_out = lax.psum_scatter(halves, "expert", scatter_dimension=0, tiled=True)
     return (attn_values, moe_out)

time: 140 us -> 135 us (0.964)
  matrix products: 39.4 us -> 4.04 us
  Pallas kernels: 87.6 us -> 120 us
  other arithmetic: 4.92 us -> 1.51 us
    dot_general x3 -> x0, matrix products: 34.6 us -> none  [the longest x1 13.4 us: expert_block(): partial_out = jnp.dot(hidden, w_down[0], preferred_element_type=jnp.float32)]
    pallas_call x1, Pallas kernels: 45.5 us -> 64.3 us  [scatter_rows(): pl.pallas_call(scatter_kernel, out_shape=jax.ShapeDtypeStruct((rows, widt...]
    pallas_call x1, Pallas kernels: 42.1 us -> 56.1 us  [gather_rows(): pl.pallas_call(partial(gather_kernel, experts), out_shape=(jax.ShapeDtype...]
    unnamed x21, local copies, waits for them, and re-layouts: 3.46 us -> 5.51 us
    reduce_sum x2 -> x0, other arithmetic: 1.41 us -> none  [the longest x1 0.71 us: expert_shares(): return jnp.sum(jnp.where(hot, share[:, :, None], 0.0), axis=1)]
where the time goes in v3:
time: 135 us
  Pallas kernels  120 us (89%)
  local copies, waits for them, and re-layouts  8.1 us (6%)
  matrix products  4.04 us (3%)
  other arithmetic  1.51 us (1%)
    pallas_call x1, Pallas kernels, scatter_rows(): pl.pallas_call(scatter_kernel, out_shape=jax.ShapeDtypeStruct((rows, widt...  64.3 us
    pallas_call x1, Pallas kernels, gather_rows(): pl.pallas_call(partial(gather_kernel, experts), out_shape=(jax.ShapeDtype...  56.1 us
    unnamed x21, local copies, waits for them, and re-layouts  5.51 us

profile of v3, /device:TPU:0, one launch (start us, length us, event | category | flops | bytes accessed | tf_op | source)
XLA Modules:
  0.0 134.8 jit_solution(2644303506287062549)
XLA Ops:
  0.6 0.0 copy-start
  0.6 0.8 compare_and_fusion
  1.4 1.8 %gather_fusion = bf16[32,16,576]{2,1,0:T(8,128)(2,1)S(1)} fusion(bf16[32,16,576]{2,1,0:T(8,128)(2,1)} %param.15, s32[1024]{0:T(1024)S(1)} %pad_clamp_fusion), kind=kCustom, calls=%fused_computation | custom fusion | bytes 1179776 | tf_op jit(solution)/shard_map/jit(_take)/gather | solution.py:426
  3.2 0.0 copy-start.8
  3.2 0.0 copy-start.7
  3.2 0.1 broadcast_in_dim.36
  3.3 0.1 broadcast_select_fusion
  3.4 0.0 copy-done
  3.5 0.5 fusion.21
  4.0 0.0 copy-start.4
  4.0 0.0 copy-done.8
  4.0 0.1 iota_compare_fusion
  4.1 0.4 copy-done.7
  4.5 0.7 fusion.20
  5.2 0.0 copy-done.4
  5.2 0.5 fusion.15
  5.7 0.1 fusion.12
  5.8 0.4 fusion.8
  6.2 0.0 copy-start.3
  6.2 0.8 fusion.4
  7.0 0.5 add_convert_fusion
  7.5 0.9 copy-done.3
  8.4 0.0 copy-start.5
  8.4 0.0 copy-start.6
  8.4 1.1 fusion.2
  9.5 0.7 copy.35
  10.2 0.0 copy-done.5
  10.2 0.7 copy.22.routes_ref
  10.9 0.0 copy-done.6
  10.9 0.7 copy.23.scores_ref
  11.6 56.1 %shard_map.140 = (bf16[512,1024]{1,0:T(8,128)(2,1)}, f32[512,128]{1,0:T(8,128)}) custom-call(bf16[32,3584]{1,0:T(8,128)(2,1)} %x_ref.1, s32[32,8]{1,0:T(8,128)} %copy.22.routes_ref, f32[32,8]{1,0:T(8,128)} %copy.23.scores_ref, bf16[1,7168,1024]{2,1,0:T(8,128)(2,1)} %gate_ref.1, bf16[1,7168,1024]{2,1,0:T(8,128)(2,1)} %up_ref.1), custom_call_target="tpu_custom_call" | custom-call | tf_op jit(solution)/shard_map/pallas_call | solution.py:229
  67.7 0.0 copy-start.1
  67.7 1.2 copy-done.1
  68.9 0.0 copy-start.2
  68.9 0.9 copy-done.2
  69.9 64.3 %shard_map.141 = bf16[32,3584]{1,0:T(8,128)(2,1)S(1)} custom-call(bf16[512,1024]{1,0:T(8,128)(2,1)S(1)} %copy-done.1, f32[512,128]{1,0:T(8,128)S(1)} %copy-done.2, bf16[1,1024,7168]{2,1,0:T(8,128)(2,1)} %down_ref.1), custom_call_target="tpu_custom_call" | custom-call | tf_op jit(solution)/shard_map/pallas_call | solution.py:378
  134.1 0.7 copy.37
  (4 shorter events, 0.0 us)
Async XLA Ops:
  0.6 2.8 %copy-start = (bf16[32,32,576]{2,1,0:T(8,128)(2,1)S(1)}, bf16[32,32,576]{2,1,0:T(8,128)(2,1)}, u32[]{:S(2)}) copy-start(bf16[32,32,576]{2,1,0:T(8,128)(2,1)} %param.13) | copy-start | bytes 3538948
  3.2 0.8 copy-start.8
  3.2 1.3 copy-start.7
  4.0 1.2 copy-start.4
  6.2 2.2 %copy-start.3 = (bf16[32,512,128]{2,1,0:T(8,128)(2,1)S(1)}, bf16[32,512,128]{2,1,0:T(8,128)(2,1)}, u32[]{:S(2)}) copy-start(bf16[32,512,128]{2,1,0:T(8,128)(2,1)} %param.19) | copy-start | bytes 12582916
  8.4 1.8 %copy-start.5 = (s32[32,8]{0,1:T(8,128)S(1)}, s32[32,8]{0,1:T(8,128)}, u32[]{:S(2)}) copy-start(s32[32,8]{0,1:T(8,128)} %param.21) | copy-start | bytes 3076
  8.4 2.5 %copy-start.6 = (f32[32,8]{0,1:T(8,128)S(1)}, f32[32,8]{0,1:T(8,128)}, u32[]{:S(2)}) copy-start(f32[32,8]{0,1:T(8,128)} %param.22) | copy-start | bytes 3076
  67.7 1.2 copy-start.1
  68.9 0.9 copy-start.2

commit v4 on v3

--- a/solution.py
+++ b/solution.py
@@ -113,7 +113,7 @@
 
 
 gather_copies = 62
-scatter_copies = 43
+scatter_copies = 59
 
 
 def gather_kernel(
@@ -258,7 +258,6 @@
     halves = (pl.ds(0, half), pl.ds(half, half))
     links = Links(send_sem, recv_sem)
     order = (1, 3, 2, 0)
-    pieces = ((1, 1), (1, 0), (0, 1), (0, 0))
     by_core, by_x, by_y, by_x2, by_y2, by_z = {}, {}, {}, {}, {}, {}
 
     def place(d, fx, fy, fc):
@@ -271,23 +270,28 @@
             total = total + value.astype(jnp.float32)
         return total.astype(jnp.bfloat16)
 
-    def add_core(d, fx, fy):
-        by_core[d, fx, fy].wait_recv()
+    def add_core(d, fx, fy, h):
+        by_core[d, fx, fy, h].wait_recv()
         row, column = place(d, fx, fy, 0)
-        for h in range(2):
-            first = pl.multiple_of(column + h * half, 128)
-            mine = p_ref[pl.ds(row, rows), pl.ds(first, half)]
-            sums[d, fx, fy, :, halves[h]] = wide(sums[d, fx, fy, :, halves[h]], mine)
-
-    def first_hop(d):
-        add_core(d, 1, 1)
+        first = pl.multiple_of(column + h * half, 128)
+        mine = p_ref[pl.ds(row, rows), pl.ds(first, half)]
+        sums[d, fx, fy, :, halves[h]] = wide(sums[d, fx, fy, :, halves[h]], mine)
+
+    def first_hop_far(d):
+        add_core(d, 1, 1, 0)
         by_x[d, 1] = links.send(sums.at[d, 1, 1, :, halves[0]], from_x.at[d, 1], fx=1)
+        add_core(d, 1, 1, 1)
         by_y[d, 1] = links.send(sums.at[d, 1, 1, :, halves[1]], from_y.at[d, 1], fy=1)
-        add_core(d, 1, 0)
+        add_core(d, 1, 0, 0)
         by_x[d, 0] = links.send(sums.at[d, 1, 0, :, halves[0]], from_x.at[d, 0], fx=1)
-        add_core(d, 0, 1)
+        add_core(d, 1, 0, 1)
+
+    def first_hop_near(d):
+        add_core(d, 0, 1, 1)
         by_y[d, 0] = links.send(sums.at[d, 0, 1, :, halves[1]], from_y.at[d, 0], fy=1)
-        add_core(d, 0, 0)
+        add_core(d, 0, 1, 0)
+        add_core(d, 0, 0, 0)
+        add_core(d, 0, 0, 1)
 
     def second_hop(d):
         by_x[d, 1].wait_recv()
@@ -311,50 +315,56 @@
         if d:
             by_z[d] = links.send(sums.at[d, 0, 0], from_z.at[d - 1], dz=d)
 
-    parts = [pl.ds(part * half, half) for part in range(4)]
-    loads = [
-        pltpu.make_async_copy(
-            down_ref.at[0, :, parts[part]], down_held.at[:, parts[part]], local_sem.at[part]
-        )
-        for part in range(4)
-    ]
-
-    def produce(d):
-        group = pl.ds(pl.multiple_of((links.z + d) % 4 * (4 * rows), 4 * rows), 4 * rows)
-        shares = shares_ref[group, :]
-        lanes = lax.broadcasted_iota(jnp.int32, shares.shape, 1)
-        share = jnp.sum(
-            jnp.where(lanes == lax.axis_index("expert"), shares, 0.0), axis=1, keepdims=True
-        )
-        for part in range(4):
-            if d == order[0]:
-                loads[part].wait()
-
-            @pl.loop(0, half // 256)
-            def _(tile):
-                columns = pl.ds(pl.multiple_of(part * half + tile * 256, 256), 256)
-                product = jnp.dot(
-                    hidden_ref[group, :], down_held[:, columns], preferred_element_type=jnp.float32
+    parts = ((1, 0), (1, 1), (0, 1), (0, 0))
+
+    def part_start(fx, h):
+        return pl.multiple_of(links.flip(links.x, fx) * width + h * half, 256)
+
+    loads = {}
+    for i, part in enumerate(parts):
+        columns = pl.ds(part_start(*part), half)
+        loads[part] = pltpu.make_async_copy(
+            down_ref.at[0, :, columns], down_held.at[:, columns], local_sem.at[i]
+        )
+        loads[part].start()
+    shares = shares_ref[...]
+    lanes = lax.broadcasted_iota(jnp.int32, shares.shape, 1)
+    share = jnp.sum(
+        jnp.where(lanes == lax.axis_index("expert"), shares, 0.0), axis=1, keepdims=True
+    )
+
+    def produce(fx, h):
+        loads[fx, h].wait()
+        first = part_start(fx, h)
+
+        @pl.loop(0, half // 256)
+        def _(tile):
+            columns = pl.ds(pl.multiple_of(first + tile * 256, 256), 256)
+            product = jnp.dot(
+                hidden_ref[...], down_held[:, columns], preferred_element_type=jnp.float32
+            )
+            p_ref[:, columns] = (product * share).astype(p_ref.dtype)
+
+        for d in order:
+            for fy in (1, 0):
+                row, _ = place(d, fx, fy, 1)
+                by_core[d, fx, fy, h] = links.send(
+                    p_ref.at[pl.ds(row, rows), pl.ds(first, half)],
+                    sums.at[d, fx, fy, :, halves[h]],
+                    fc=1,
                 )
-                p_ref[group, columns] = (product * share).astype(p_ref.dtype)
-
-        for fx, fy in pieces:
-            row, column = place(d, fx, fy, 1)
-            by_core[d, fx, fy] = links.send(
-                p_ref.at[pl.ds(row, rows), pl.ds(pl.multiple_of(column, 128), width)],
-                sums.at[d, fx, fy],
-                fc=1,
-            )
-
-    for load in loads:
-        load.start()
+
     links.greet()
-    produce(order[0])
+    for part in parts[:3]:
+        produce(*part)
+    for d in order[:2]:
+        first_hop_far(d)
+    produce(*parts[3])
     for step in range(6):
-        if step + 1 < 4:
-            produce(order[step + 1])
+        if 2 <= step < 4:
+            first_hop_far(order[step])
         if step < 4:
-            first_hop(order[step])
+            first_hop_near(order[step])
         if 0 <= step - 1 < 4:
             second_hop(order[step - 1])
         if step >= 2:

time: 135 us -> 128 us (0.948)
  Pallas kernels: 120 us -> 113 us
    pallas_call x1, Pallas kernels: 64.3 us -> 56.6 us  [scatter_rows(): pl.pallas_call(scatter_kernel, out_shape=jax.ShapeDtypeStruct((rows, widt...]
where the time goes in v4:
time: 128 us; the launch traced here: 127 us
  Pallas kernels  113 us (88%)
  local copies, waits for them, and re-layouts  8.1 us (6%)
  matrix products  4.04 us (3%)
  other arithmetic  1.51 us (1%)
    pallas_call x1, Pallas kernels, scatter_rows(): pl.pallas_call(scatter_kernel, out_shape=jax.ShapeDtypeStruct((rows, widt...  56.6 us
    pallas_call x1, Pallas kernels, gather_rows(): pl.pallas_call(partial(gather_kernel, experts), out_shape=(jax.ShapeDtype...  56.1 us
    unnamed x21, local copies, waits for them, and re-layouts  5.51 us

profile of v4, /device:TPU:0, one launch (start us, length us, event | category | flops | bytes accessed | tf_op | source)
XLA Modules:
  0.0 127.2 jit_solution(13669582358371279203)
XLA Ops:
  0.6 0.0 copy-start
  0.6 0.8 compare_and_fusion
  1.4 1.8 %gather_fusion = bf16[32,16,576]{2,1,0:T(8,128)(2,1)S(1)} fusion(bf16[32,16,576]{2,1,0:T(8,128)(2,1)} %param.15, s32[1024]{0:T(1024)S(1)} %pad_clamp_fusion), kind=kCustom, calls=%fused_computation | custom fusion | bytes 1179776 | tf_op jit(solution)/shard_map/jit(_take)/gather | solution.py:436
  3.2 0.0 copy-start.8
  3.2 0.0 copy-start.7
  3.2 0.1 broadcast_in_dim.36
  3.3 0.1 broadcast_select_fusion
  3.4 0.0 copy-done
  3.5 0.5 fusion.21
  4.0 0.0 copy-start.4
  4.0 0.0 copy-done.8
  4.0 0.1 iota_compare_fusion
  4.1 0.4 copy-done.7
  4.5 0.7 fusion.20
  5.2 0.0 copy-done.4
  5.2 0.5 fusion.15
  5.7 0.1 fusion.12
  5.8 0.4 fusion.8
  6.2 0.0 copy-start.3
  6.2 0.8 fusion.4
  7.0 0.5 add_convert_fusion
  7.5 0.9 copy-done.3
  8.4 0.0 copy-start.5
  8.4 0.0 copy-start.6
  8.4 1.1 fusion.2
  9.5 0.7 copy.35
  10.2 0.0 copy-done.5
  10.2 0.7 copy.22.routes_ref
  10.9 0.0 copy-done.6
  10.9 0.7 copy.23.scores_ref
  11.6 56.1 %shard_map.140 = (bf16[512,1024]{1,0:T(8,128)(2,1)}, f32[512,128]{1,0:T(8,128)}) custom-call(bf16[32,3584]{1,0:T(8,128)(2,1)} %x_ref.1, s32[32,8]{1,0:T(8,128)} %copy.22.routes_ref, f32[32,8]{1,0:T(8,128)} %copy.23.scores_ref, bf16[1,7168,1024]{2,1,0:T(8,128)(2,1)} %gate_ref.1, bf16[1,7168,1024]{2,1,0:T(8,128)(2,1)} %up_ref.1), custom_call_target="tpu_custom_call" | custom-call | tf_op jit(solution)/shard_map/pallas_call | solution.py:229
  67.7 0.0 copy-start.1
  67.7 1.2 copy-done.1
  68.9 0.0 copy-start.2
  68.9 0.9 copy-done.2
  69.9 56.6 %shard_map.141 = bf16[32,3584]{1,0:T(8,128)(2,1)S(1)} custom-call(bf16[512,1024]{1,0:T(8,128)(2,1)S(1)} %copy-done.1, f32[512,128]{1,0:T(8,128)S(1)} %copy-done.2, bf16[1,1024,7168]{2,1,0:T(8,128)(2,1)} %down_ref.1), custom_call_target="tpu_custom_call" | custom-call | tf_op jit(solution)/shard_map/pallas_call | solution.py:388
  126.5 0.7 copy.37
  (4 shorter events, 0.0 us)
Async XLA Ops:
  0.6 2.8 %copy-start = (bf16[32,32,576]{2,1,0:T(8,128)(2,1)S(1)}, bf16[32,32,576]{2,1,0:T(8,128)(2,1)}, u32[]{:S(2)}) copy-start(bf16[32,32,576]{2,1,0:T(8,128)(2,1)} %param.13) | copy-start | bytes 3538948
  3.2 0.8 copy-start.8
  3.2 1.3 %copy-start.7 = (bf16[4,256,576]{1,2,0:T(8,128)(2,1)S(1)}, bf16[4,256,576]{1,2,0:T(8,128)(2,1)}, u32[]{:S(2)}) copy-start(bf16[4,256,576]{1,2,0:T(8,128)(2,1)} %param.14) | copy-start | bytes 3538948
  4.0 1.2 copy-start.4
  6.2 2.2 %copy-start.3 = (bf16[32,512,128]{2,1,0:T(8,128)(2,1)S(1)}, bf16[32,512,128]{2,1,0:T(8,128)(2,1)}, u32[]{:S(2)}) copy-start(bf16[32,512,128]{2,1,0:T(8,128)(2,1)} %param.19) | copy-start | bytes 12582916
  8.4 1.8 %copy-start.5 = (s32[32,8]{0,1:T(8,128)S(1)}, s32[32,8]{0,1:T(8,128)}, u32[]{:S(2)}) copy-start(s32[32,8]{0,1:T(8,128)} %param.21) | copy-start | bytes 3076
  8.4 2.5 %copy-start.6 = (f32[32,8]{0,1:T(8,128)S(1)}, f32[32,8]{0,1:T(8,128)}, u32[]{:S(2)}) copy-start(f32[32,8]{0,1:T(8,128)} %param.22) | copy-start | bytes 3076
  67.7 1.2 copy-start.1
  68.9 0.9 copy-start.2
